TPU v7x, 512 devices: a whole 4x8x8 slice. The times are simulated.
512 devices in a mesh: space: 16 (over z, core), member: 8 (over y), tm: 4 (over x).
Axes of the slice: x: 4, y: 8, z: 8, core: 2. Of those that a mesh axis runs over, the one named last changes fastest.
Arguments:
- ens_pert: bfloat16 [8, 128, 131072], P('tm', 'member', 'space'), may hold values from -6 to 6
- weights: float32 [128, 512], P('member', 'space'), may hold values from -6 to 6
- foot_block: int32 [8, 16, 16, 8, 32], P('tm', 'space'), may hold values from 0 to 31
- foot_offset: int32 [8, 16, 16, 8, 32], P('tm', 'space'), may hold values from 0 to 255
- innovation: float32 [8, 16, 8, 16, 32], P('tm', 'space', 'member'), may hold values from -6 to 6
- inv_var: float32 [8, 16, 8, 16, 32], P('tm', 'space', 'member'), may hold values from 0.25 to 2.5
- obs_count: int32 [8, 16, 8, 16], P('tm', 'space', 'member'), may hold values from 1 to 32, as said below
Outputs:
- gradient: float32 [128, 512], P('member', 'space')
Inputs may be any that keep to these rules, and one draw needn't show every extreme that they name: `obs_count`: live slots come first among the 32 slots; in every time slot one destination tile has all 32 slots live from every owner.
All inputs are finite; a program needn't handle non-finite values.
Results may differ from a plain program's by a relative error of at most 0.0029.
Values sent between devices are 32-bit elements; how exact they have to be, the bound alone decides.
No kernel may reach another device: no remote copies, remote signals or barrier semaphores. Data moves between devices by JAX's collectives and lax.ppermute only.
A program may use at most 64 MiB of HBM per device.

v0:
```python
import math
import jax
import jax.numpy as jnp
from jax import lax
from jax.sharding import PartitionSpec as P

BLOCK = 256


def split_pair(values, axis_at):
    upper = lax.optimization_barrier(values.astype(jnp.bfloat16))
    lower = (values - upper.astype(jnp.float32)).astype(jnp.bfloat16)
    return jnp.concatenate([upper, lower], axis=axis_at)


def shards(ens_pert, weights, foot_block, foot_offset, innovation, inv_var, obs_count):
    tile_count = lax.axis_size("space")
    group_count = lax.axis_size("member")
    slot_count, members, cell_dev = ens_pert.shape
    capacity = foot_block.shape[-1]
    blk_dev = cell_dev // BLOCK
    norm_scale = 1.0 / math.sqrt(members * group_count - 1)
    pert_blocks = ens_pert.reshape(slot_count, members, blk_dev, BLOCK)
    weights_rounded = weights.astype(jnp.bfloat16)
    partial_field = norm_scale * jnp.einsum(
        "tmbc,mb->tbc", pert_blocks, weights_rounded, preferred_element_type=jnp.float32
    )
    split_field = split_pair(partial_field, 1)
    block_rows = jnp.transpose(foot_block.reshape(slot_count, tile_count, -1), (1, 0, 2))
    offset_rows = jnp.transpose(foot_offset.reshape(slot_count, tile_count, -1), (1, 0, 2))
    block_iota = lax.broadcasted_iota(jnp.int32, (1, blk_dev, 1), 1)
    offset_iota = lax.broadcasted_iota(jnp.int32, (1, 1, BLOCK), 2)

    def pick_tile(pair):
        blk_ids, off_ids = pair
        off_hot = (off_ids[:, :, None] == offset_iota).astype(jnp.bfloat16)
        proj = jnp.einsum("tjc,tkc->tjk", split_field, off_hot, preferred_element_type=jnp.float32)
        value = proj[:, :blk_dev] + proj[:, blk_dev:]
        chosen = jnp.where(blk_ids[:, None, :] == block_iota, value, jnp.zeros_like(value))
        return jnp.sum(chosen, axis=1)

    picked = jnp.transpose(lax.map(pick_tile, (block_rows, offset_rows)), (1, 0, 2))
    arrived_vals = lax.all_to_all(
        picked.reshape(slot_count, tile_count * group_count, capacity),
        ("space", "member"),
        split_axis=1,
        concat_axis=1,
        tiled=True,
    )
    model_obs = jnp.sum(arrived_vals.reshape(slot_count, tile_count, group_count, capacity), axis=2)
    innov_local = innovation.reshape(slot_count, tile_count, capacity)
    obs_weight = inv_var.reshape(slot_count, tile_count, capacity)
    counts = obs_count.reshape(slot_count, tile_count, 1)
    is_live = lax.broadcasted_iota(jnp.int32, (slot_count, tile_count, capacity), 2) < counts
    residual = jnp.where(
        is_live, obs_weight * (model_obs - innov_local), jnp.zeros_like(innov_local)
    )
    residual = residual.reshape(slot_count, 1, 1, tile_count, capacity)
    spread = lax.all_gather(residual, "member", axis=2, tiled=True)
    arrived = lax.all_to_all(spread, "space", split_axis=3, concat_axis=1, tiled=True)
    arrived_rows = jnp.transpose(arrived.reshape(slot_count, tile_count, -1), (1, 0, 2))

    def add_tile(total, triple):
        blk_ids, off_ids, values = triple
        off_hot = (off_ids[:, :, None] == offset_iota).astype(jnp.bfloat16)
        placed = jnp.where(
            blk_ids[:, None, :] == block_iota, values[:, None, :], jnp.zeros((), jnp.float32)
        )
        both = split_pair(placed, 1)
        part_sum = jnp.einsum("tjk,tkc->tjc", both, off_hot, preferred_element_type=jnp.float32)
        return (total + (part_sum[:, :blk_dev] + part_sum[:, blk_dev:]), None)

    start_total = jnp.zeros((slot_count, blk_dev, BLOCK), jnp.float32)
    adjoint, _ = lax.scan(add_tile, start_total, (block_rows, offset_rows, arrived_rows))
    adjoint_rounded = adjoint.astype(jnp.bfloat16)
    local_grad = jnp.einsum(
        "tmbc,tbc->mb", pert_blocks, adjoint_rounded, preferred_element_type=jnp.float32
    )
    summed = lax.psum(local_grad, "tm")
    return weights + norm_scale * summed


def solution(mesh):
    in_specs = (
        P("tm", "member", "space"),
        P("member", "space"),
        P("tm", "space", None, None, None),
        P("tm", "space", None, None, None),
        P("tm", "space", "member", None, None),
        P("tm", "space", "member", None, None),
        P("tm", "space", "member", None),
    )
    out_specs = P("member", "space")
    return jax.shard_map(shards, mesh=mesh, in_specs=in_specs, out_specs=out_specs, check_vma=False)
```

profile of v0, /device:TPU:1, one launch (start us, length us, event | category | flops | bytes accessed | tf_op | source)
XLA Modules:
  0.0 95.3 jit_solution(16273810836954491873)
XLA Ops:
  0.0 0.7 convert_bitcast_fusion.1
  0.8 1.2 %fusion.21 = f32[32,1,2,256]{3,1,2,0:T(1,128)S(1)} fusion(bf16[16,32,1,1]{0,2,3,1:T(2,128)(2,1)S(1)} %copy.38, bf16[2,2,32,8,256]{4,3,2,1,0:T(8,128)(2,1)} %bitcast.84), kind=kOutput, calls=%fused_computation.32 | convolution fusion | flops 524288 | bytes 590848 | tf_op jit(solution)/shard_map/tmbc,mb->tbc/dot_general | solution.py:25
  2.1 0.8 copy-done.1
  3.2 5.8 %while.22 = (s32[]{:T(128)}, f32[16,2,256]{2,1,0:T(2,128)S(1)}, s32[16,2,256]{2,1,0:T(2,128)S(1)}, s32[16,2,256]{2,1,0:T(2,128)S(1)}, bf16[2,64,256]{2,1,0:T(8,128)(2,1)S(1)}, /*index=5*/s32[]{:T(128)}) while((s32[]{:T(128)}, f32[16,2,256]{2,1,0:T(2,128)S(1)}, s32[16,2,256]{2,1,0:T(2,128)S(1)}, s32[16,2,256]{2,1,0:T(2,128)S(1)}, ...), condition=%wide.region_2.3_spmd.clone, body=%wide.region_0.2_spmd.clone.sunk | while | flops 16973312 | bytes 346189 | solution.py:42
  9.1 0.8 copy.33
  9.9 18.4 %all-to-all-start = ((f32[2,128,32]{2,0,1:T(2,128)}), f32[2,128,32]{2,0,1:T(2,128)S(1)}, u32[]{:S(2)}, u32[]{:S(2)}) async-start(f32[2,128,32]{2,0,1:T(2,128)} %copy.33), calls=%async_computation | async-start | bytes 262144 | tf_op jit(solution)/shard_map/all_to_all | solution.py:43
  28.3 0.7 copy-done.6
  29.1 11.8 %all-to-all-done = f32[2,128,32]{2,0,1:T(2,128)S(1)} async-done(((f32[2,128,32]{2,0,1:T(2,128)}), f32[2,128,32]{2,0,1:T(2,128)S(1)}, u32[]{:S(2)}, u32[]{:S(2)}) %all-to-all-start) | async-done | bytes 32800 | tf_op jit(solution)/shard_map/all_to_all | solution.py:43
  41.0 18.2 %all_gather.3 = f32[2,1,8,16,32]{4,3,1,0,2:T(8,128)S(1)} all-gather(f32[2,1,1,16,32]{4,3,1,0,2:T(8,128)S(1)} %copy.36), channel_id=1, replica_groups=mesh['space'=16,'member'=8,'tm'=4] {'member'}, dimensions={2}, use_global_device_ids=true | all-gather | bytes 36864 | tf_op jit(solution)/shard_map/all_gather | solution.py:59
  59.4 0.7 reshape.54
  60.1 10.0 %all-to-all-start.1 = ((f32[16,1,512]{2,1,0:T(1,128)}), f32[16,1,512]{2,1,0:T(1,128)S(1)}, u32[]{:S(2)}, u32[]{:S(2)}) async-start(f32[16,1,512]{2,1,0:T(1,128)} %reshape.54), calls=%async_computation.1 | async-start | bytes 65536 | tf_op jit(solution)/shard_map/all_to_all | solution.py:60
  70.1 7.5 %all-to-all-done.1 = f32[16,1,512]{2,1,0:T(1,128)S(1)} async-done(((f32[16,1,512]{2,1,0:T(1,128)}), f32[16,1,512]{2,1,0:T(1,128)S(1)}, u32[]{:S(2)}, u32[]{:S(2)}) %all-to-all-start.1) | async-done | bytes 32800 | tf_op jit(solution)/shard_map/all_to_all | solution.py:60
  77.6 0.5 broadcast.27
  78.1 0.7 reduce
  79.0 6.6 %while.23 = (s32[]{:T(128)}, f32[2,32,256]{2,1,0:T(8,128)S(1)}, s32[16,2,256]{2,1,0:T(2,128)S(1)}, f32[16,2,256]{2,1,0:T(2,128)S(1)}, s32[16,2,256]{2,1,0:T(2,128)S(1)}, /*index=5*/s32[]{:T(128)}, s32[]{:T(128)}) while((s32[]{:T(128)}, f32[2,32,256]{2,1,0:T(8,128)S(1)}, s32[16,2,256]{2,1,0:T(2,128)S(1)}, ...), condition=%wide.region_5.6_spmd.clone, body=%wide.region_4.5_spmd.clone.sunk | while | flops 17203200 | bytes 579679 | solution.py:74
  79.1 0.3 fusion.40
  83.2 0.3 fusion.40
  83.7 0.3 fusion.40
  84.1 0.3 fusion.40
  84.5 0.3 fusion.40
  84.9 0.3 fusion.40
  85.3 0.3 fusion.40
  86.0 8.7 %psum.7 = f32[16,32]{1,0:T(8,128)S(1)} all-reduce(f32[16,32]{1,0:T(8,128)S(1)} %bitcast.88), channel_id=1, replica_groups=mesh['space'=16,'member'=8,'tm'=4] {'tm'}, use_global_device_ids=true, to_apply=%region_6.7 | all-reduce | flops 512 | bytes 4096 | tf_op jit(solution)/shard_map/psum | solution.py:79
  94.7 0.6 multiply_add_fusion
  (187 shorter events, 10.2 us)
Async XLA Ops:
  2.1 0.9 copy-start.1
  2.1 1.0 %copy-start.2 = (s32[2,1,16,8,32]{4,3,2,1,0:T(8,128)S(1)}, s32[2,1,16,8,32]{4,3,2,1,0:T(8,128)}, u32[]{:S(2)}) copy-start(s32[2,1,16,8,32]{4,3,2,1,0:T(8,128)} %param.14) | copy-start | bytes 98308
  9.9 31.0 %all-to-all-start = ((f32[2,128,32]{2,0,1:T(2,128)}), f32[2,128,32]{2,0,1:T(2,128)S(1)}, u32[]{:S(2)}, u32[]{:S(2)}) async-start(f32[2,128,32]{2,0,1:T(2,128)} %copy.33), calls=%async_computation | async-start | bytes 262144 | tf_op jit(solution)/shard_map/all_to_all | solution.py:43
  28.3 0.7 copy-start.6
  29.1 11.8 %copy-start.4 = (f32[2,1,1,16,32]{4,3,2,1,0:T(8,128)S(1)}, f32[2,1,1,16,32]{4,3,2,1,0:T(8,128)}, u32[]{:S(2)}) copy-start(f32[2,1,1,16,32]{4,3,2,1,0:T(8,128)} %param.16) | copy-start | bytes 12292
  29.1 11.8 %copy-start.5 = (f32[2,1,1,16,32]{4,3,2,1,0:T(8,128)S(1)}, f32[2,1,1,16,32]{4,3,2,1,0:T(8,128)}, u32[]{:S(2)}) copy-start(f32[2,1,1,16,32]{4,3,2,1,0:T(8,128)} %param.15) | copy-start | bytes 12292
  60.1 17.5 %all-to-all-start.1 = ((f32[16,1,512]{2,1,0:T(1,128)}), f32[16,1,512]{2,1,0:T(1,128)S(1)}, u32[]{:S(2)}, u32[]{:S(2)}) async-start(f32[16,1,512]{2,1,0:T(1,128)} %reshape.54), calls=%async_computation.1 | async-start | bytes 65536 | tf_op jit(solution)/shard_map/all_to_all | solution.py:60
  79.0 6.6 %copy-start = (bf16[2,16,8192]{2,1,0:T(8,128)(2,1)S(1)}, bf16[2,16,8192]{2,1,0:T(8,128)(2,1)}, u32[]{:S(2)}) copy-start(bf16[2,16,8192]{2,1,0:T(8,128)(2,1)} %param.11) | copy-start | bytes 1572868
  86.0 8.7 %copy-start.3 = (f32[16,32]{1,0:T(8,128)S(1)}, f32[16,32]{1,0:T(8,128)}, u32[]{:S(2)}) copy-start(f32[16,32]{1,0:T(8,128)} %param.12) | copy-start | bytes 6148
where the time goes:
time: 95.7 us; the launch traced here: 95.3 us
  starting transfers between devices  28.4 us (30%)
  blocking collectives  26.9 us (28%)
  waiting for transfers between devices  19.2 us (20%)
  matrix products  10.3 us (11%)
  local copies, waits for them, and re-layouts  5.06 us (5%)
  other arithmetic  3.52 us (4%)
  loops' own time  1.59 us (2%)
    all_to_all x1, starting transfers between devices, shards(): lax.all_to_all(picked.reshape(slot_count, tile_count * group_count, capac...  18.4 us
    all_gather x1, blocking collectives, shards(): spread = lax.all_gather(residual, 'member', axis=2, tiled=True)  18.2 us
    all_to_all x1, waiting for transfers between devices, shards(): lax.all_to_all(picked.reshape(slot_count, tile_count * group_count, capac...  11.8 us
    all_to_all x1, starting transfers between devices, shards(): lax.all_to_all(spread, 'space', split_axis=3, concat_axis=1, tiled=True)  10 us
    psum x1, blocking collectives, shards(): summed = lax.psum(local_grad, 'tm')  8.7 us
    all_to_all x1, waiting for transfers between devices, shards(): lax.all_to_all(spread, 'space', split_axis=3, concat_axis=1, tiled=True)  7.48 us
    dot_general x16, matrix products, add_tile(): jnp.einsum('tjk,tkc->tjc', both, off_hot, preferred_element_type=jnp.floa...  4.45 us
    dot_general x16, matrix products, pick_tile(): jnp.einsum('tjc,tkc->tjk', split_field, off_hot, preferred_element_type=j...  4.35 us
  transfers between devices with their start and end apart: 2, of which 2 were waited for; matrix products, arithmetic and copies ran while one was open for 0% of the time, Pallas kernels for 0%

commit v1 on v0

--- a/solution.py
+++ b/solution.py
@@ -5,6 +5,11 @@
 from jax.sharding import PartitionSpec as P
 
 BLOCK = 256
+
+
+def tiled_gather(value, axis, dim):
+    copies = jnp.concatenate([value] * lax.axis_size(axis), axis=dim)
+    return lax.all_to_all(copies, axis, dim, dim, tiled=True)
 
 
 def split_pair(values, axis_at):
@@ -56,7 +61,7 @@
         is_live, obs_weight * (model_obs - innov_local), jnp.zeros_like(innov_local)
     )
     residual = residual.reshape(slot_count, 1, 1, tile_count, capacity)
-    spread = lax.all_gather(residual, "member", axis=2, tiled=True)
+    spread = tiled_gather(residual, "member", 2)
     arrived = lax.all_to_all(spread, "space", split_axis=3, concat_axis=1, tiled=True)
     arrived_rows = jnp.transpose(arrived.reshape(slot_count, tile_count, -1), (1, 0, 2))
 

time: 95.7 us -> 83.1 us (0.87)
  blocking collectives: 26.9 us -> 17.9 us
  starting transfers between devices: 28.4 us -> 23.8 us
    all_gather x1 -> x0, blocking collectives: 18.2 us -> none  [shards(): spread = lax.all_gather(residual, 'member', axis=2, tiled=True)]
    all_to_all x0 -> x1, blocking collectives: none -> 9.25 us  [tiled_gather(): return lax.all_to_all(copies, axis, dim, dim, tiled=True)]
    all_to_all x1, starting transfers between devices: 10 us -> 5.34 us  [shards(): lax.all_to_all(spread, 'space', split_axis=3, concat_axis=1, tiled=True)]
    unnamed x16 -> x19, local copies, waits for them, and re-layouts: 2.36 us -> 2.71 us
where the time goes in v1:
time: 83.1 us; the launch traced here: 82.7 us
  starting transfers between devices  23.8 us (29%)
  waiting for transfers between devices  19.2 us (23%)
  blocking collectives  17.9 us (22%)
  matrix products  10.3 us (12%)
  local copies, waits for them, and re-layouts  5.4 us (6%)
  other arithmetic  4.19 us (5%)
  loops' own time  1.59 us (2%)
    all_to_all x1, starting transfers between devices, shards(): lax.all_to_all(picked.reshape(slot_count, tile_count * group_count, capac...  18.4 us
    all_to_all x1, waiting for transfers between devices, shards(): lax.all_to_all(picked.reshape(slot_count, tile_count * group_count, capac...  11.8 us
    all_to_all x1, blocking collectives, tiled_gather(): return lax.all_to_all(copies, axis, dim, dim, tiled=True)  9.25 us
    psum x1, blocking collectives, shards(): summed = lax.psum(local_grad, 'tm')  8.7 us
    all_to_all x1, waiting for transfers between devices, shards(): lax.all_to_all(spread, 'space', split_axis=3, concat_axis=1, tiled=True)  7.48 us
    all_to_all x1, starting transfers between devices, shards(): lax.all_to_all(spread, 'space', split_axis=3, concat_axis=1, tiled=True)  5.34 us
    dot_general x16, matrix products, add_tile(): jnp.einsum('tjk,tkc->tjc', both, off_hot, preferred_element_type=jnp.floa...  4.45 us
    dot_general x16, matrix products, pick_tile(): jnp.einsum('tjc,tkc->tjk', split_field, off_hot, preferred_element_type=j...  4.35 us
  transfers between devices with their start and end apart: 2, of which 2 were waited for; matrix products, arithmetic and copies ran while one was open for 0% of the time, Pallas kernels for 0%

profile of v1, /device:TPU:1, one launch (start us, length us, event | category | flops | bytes accessed | tf_op | source)
XLA Modules:
  0.0 82.7 jit_solution(5439320197923222274)
XLA Ops:
  0.0 0.7 convert_bitcast_fusion.1
  0.8 1.2 %fusion.21 = f32[32,1,2,256]{3,1,2,0:T(1,128)S(1)} fusion(bf16[16,32,1,1]{0,2,3,1:T(2,128)(2,1)S(1)} %copy.29, bf16[2,2,32,8,256]{4,3,2,1,0:T(8,128)(2,1)} %bitcast.89), kind=kOutput, calls=%fused_computation.32 | convolution fusion | flops 524288 | bytes 590848 | tf_op jit(solution)/shard_map/tmbc,mb->tbc/dot_general | solution.py:30
  2.1 0.8 %copy-done.1 = s32[2,1,16,8,32]{4,3,2,1,0:T(8,128)S(1)} copy-done((s32[2,1,16,8,32]{4,3,2,1,0:T(8,128)S(1)}, s32[2,1,16,8,32]{4,3,2,1,0:T(8,128)}, u32[]{:S(2)}) %copy-start.1) | copy-done | bytes 32792
  3.2 5.8 %while.22 = (s32[]{:T(128)}, f32[16,2,256]{2,1,0:T(2,128)S(1)}, s32[16,2,256]{2,1,0:T(2,128)S(1)}, s32[16,2,256]{2,1,0:T(2,128)S(1)}, bf16[2,64,256]{2,1,0:T(8,128)(2,1)S(1)}, /*index=5*/s32[]{:T(128)}) while((s32[]{:T(128)}, f32[16,2,256]{2,1,0:T(2,128)S(1)}, s32[16,2,256]{2,1,0:T(2,128)S(1)}, s32[16,2,256]{2,1,0:T(2,128)S(1)}, ...), condition=%wide.region_2.3_spmd.clone, body=%wide.region_0.2_spmd.clone.sunk | while | flops 16973312 | bytes 346189 | solution.py:47
  9.1 0.7 copy.25
  9.9 18.4 %all-to-all-start = ((f32[2,128,32]{2,0,1:T(2,128)}), f32[2,128,32]{2,0,1:T(2,128)S(1)}, u32[]{:S(2)}, u32[]{:S(2)}) async-start(f32[2,128,32]{2,0,1:T(2,128)} %copy.25), calls=%async_computation | async-start | bytes 262144 | tf_op jit(solution)/shard_map/all_to_all | solution.py:48
  28.3 0.7 copy-done.6
  29.1 11.8 %all-to-all-done = f32[2,128,32]{2,0,1:T(2,128)S(1)} async-done(((f32[2,128,32]{2,0,1:T(2,128)}), f32[2,128,32]{2,0,1:T(2,128)S(1)}, u32[]{:S(2)}, u32[]{:S(2)}) %all-to-all-start) | async-done | bytes 32800 | tf_op jit(solution)/shard_map/all_to_all | solution.py:48
  41.2 9.2 %all_to_all.25 = f32[8,1,1024]{2,1,0:T(1,128)S(1)} all-to-all(f32[8,1,1024]{2,1,0:T(1,128)S(1)} %reshape.60), channel_id=1, replica_groups=mesh['space'=16,'member'=8,'tm'=4] {'member'}, dimensions={0} | all-to-all | bytes 65536 | tf_op jit(solution)/shard_map/all_to_all | solution.py:12
  50.5 0.5 broadcast.29
  51.0 0.7 reduce
  51.9 0.7 reshape.62
  52.7 5.3 %all-to-all-start.2 = ((f32[16,1,512]{2,1,0:T(1,128)}), f32[16,1,512]{2,1,0:T(1,128)S(1)}, u32[]{:S(2)}, u32[]{:S(2)}) async-start(f32[16,1,512]{2,1,0:T(1,128)} %reshape.62), calls=%async_computation.2 | async-start | bytes 65536 | tf_op jit(solution)/shard_map/all_to_all | solution.py:65
  58.0 7.5 %all-to-all-done.2 = f32[16,1,512]{2,1,0:T(1,128)S(1)} async-done(((f32[16,1,512]{2,1,0:T(1,128)}), f32[16,1,512]{2,1,0:T(1,128)S(1)}, u32[]{:S(2)}, u32[]{:S(2)}) %all-to-all-start.2) | async-done | bytes 32800 | tf_op jit(solution)/shard_map/all_to_all | solution.py:65
  65.5 0.7 reduce.1
  66.4 6.6 %while.23 = (s32[]{:T(128)}, f32[2,32,256]{2,1,0:T(8,128)S(1)}, s32[16,2,256]{2,1,0:T(2,128)S(1)}, f32[16,2,256]{2,1,0:T(2,128)S(1)}, s32[16,2,256]{2,1,0:T(2,128)S(1)}, /*index=5*/s32[]{:T(128)}, s32[]{:T(128)}) while((s32[]{:T(128)}, f32[2,32,256]{2,1,0:T(8,128)S(1)}, s32[16,2,256]{2,1,0:T(2,128)S(1)}, ...), condition=%wide.region_5.6_spmd.clone, body=%wide.region_4.5_spmd.clone.sunk | while | flops 17203200 | bytes 579679 | solution.py:79
  67.7 0.3 fusion.41
  68.1 0.3 fusion.41
  68.6 0.3 fusion.41
  69.0 0.3 fusion.41
  69.4 0.3 fusion.41
  69.8 0.3 fusion.41
  73.4 8.7 %psum.7 = f32[16,32]{1,0:T(8,128)S(1)} all-reduce(f32[16,32]{1,0:T(8,128)S(1)} %bitcast.94), channel_id=1, replica_groups=mesh['space'=16,'member'=8,'tm'=4] {'tm'}, use_global_device_ids=true, to_apply=%region_6.7 | all-reduce | flops 512 | bytes 4096 | tf_op jit(solution)/shard_map/psum | solution.py:84
  82.1 0.6 multiply_add_fusion
  (190 shorter events, 10.8 us)
Async XLA Ops:
  2.1 0.9 %copy-start.1 = (s32[2,1,16,8,32]{4,3,2,1,0:T(8,128)S(1)}, s32[2,1,16,8,32]{4,3,2,1,0:T(8,128)}, u32[]{:S(2)}) copy-start(s32[2,1,16,8,32]{4,3,2,1,0:T(8,128)} %param.13) | copy-start | bytes 98308
  2.1 1.0 %copy-start.2 = (s32[2,1,16,8,32]{4,3,2,1,0:T(8,128)S(1)}, s32[2,1,16,8,32]{4,3,2,1,0:T(8,128)}, u32[]{:S(2)}) copy-start(s32[2,1,16,8,32]{4,3,2,1,0:T(8,128)} %param.14) | copy-start | bytes 98308
  9.9 31.0 %all-to-all-start = ((f32[2,128,32]{2,0,1:T(2,128)}), f32[2,128,32]{2,0,1:T(2,128)S(1)}, u32[]{:S(2)}, u32[]{:S(2)}) async-start(f32[2,128,32]{2,0,1:T(2,128)} %copy.25), calls=%async_computation | async-start | bytes 262144 | tf_op jit(solution)/shard_map/all_to_all | solution.py:48
  28.3 0.7 copy-start.6
  29.1 11.8 %copy-start.4 = (f32[2,1,1,16,32]{4,3,2,1,0:T(8,128)S(1)}, f32[2,1,1,16,32]{4,3,2,1,0:T(8,128)}, u32[]{:S(2)}) copy-start(f32[2,1,1,16,32]{4,3,2,1,0:T(8,128)} %param.16) | copy-start | bytes 12292
  29.1 11.8 %copy-start.5 = (f32[2,1,1,16,32]{4,3,2,1,0:T(8,128)S(1)}, f32[2,1,1,16,32]{4,3,2,1,0:T(8,128)}, u32[]{:S(2)}) copy-start(f32[2,1,1,16,32]{4,3,2,1,0:T(8,128)} %param.15) | copy-start | bytes 12292
  52.7 12.8 %all-to-all-start.2 = ((f32[16,1,512]{2,1,0:T(1,128)}), f32[16,1,512]{2,1,0:T(1,128)S(1)}, u32[]{:S(2)}, u32[]{:S(2)}) async-start(f32[16,1,512]{2,1,0:T(1,128)} %reshape.62), calls=%async_computation.2 | async-start | bytes 65536 | tf_op jit(solution)/shard_map/all_to_all | solution.py:65
  66.4 6.6 %copy-start = (bf16[2,16,8192]{2,1,0:T(8,128)(2,1)S(1)}, bf16[2,16,8192]{2,1,0:T(8,128)(2,1)}, u32[]{:S(2)}) copy-start(bf16[2,16,8192]{2,1,0:T(8,128)(2,1)} %param.11) | copy-start | bytes 1572868
  73.4 8.7 %copy-start.3 = (f32[16,32]{1,0:T(8,128)S(1)}, f32[16,32]{1,0:T(8,128)}, u32[]{:S(2)}) copy-start(f32[16,32]{1,0:T(8,128)} %param.12) | copy-start | bytes 6148
